TPU v7x, 32 devices: a whole 2x2x4 slice. The times are simulated.
32 devices in a mesh: ctx: 8 (over y, x, core), tp: 4 (over z).
Axes of the slice: x: 2, y: 2, z: 4, core: 2. Of those that a mesh axis runs over, the one named last changes fastest.
Arguments:
- queries: bfloat16 [16384, 8192], P('ctx', 'tp'), may hold values from -48 to 48
- keys: bfloat16 [16384, 1024], P(('ctx', 'tp')), may hold values from -6 to 6
- values: bfloat16 [16384, 1024], P(('ctx', 'tp')), may hold values from -6 to 6
- rope_factors: float32 [64], replicated, may hold values from 1 to 32
- doc_lengths: int32 [64], replicated, may hold values from 1 to 512, 16384 in all
- owner_map: int32 [8, 8], replicated, may hold values from 0 to 7, as said below
Outputs:
- attended: bfloat16 [16384, 8192], P('ctx', 'tp')
Inputs may be any that keep to these rules, and one draw needn't show every extreme that they name: `owner_map`: row c lists the owners of the 8 blocks of index c: they are different devices, and every device owns exactly one block of each in-device number r, so exactly 8 blocks in all.
All inputs are finite; a program needn't handle non-finite values.
Results may differ from a plain program's by a relative error of at most 0.0051.
Values may be sent and summed in bfloat16 or wider, within the bound.
A program may use at most 128 MiB of HBM per device.

v0:
```python
import math

import jax
import jax.numpy as jnp
from jax import lax
from jax.sharding import PartitionSpec as P

THETA = 500000.0


def passed_along(shard, axis, by):
    length = lax.axis_size(axis)
    pairs = [(i, i + by) for i in range(length) if 0 <= i + by < length]
    return lax.ppermute(shard, axis, pairs)


def doc_tables(lengths, positions):
    doc_ends = jnp.cumsum(lengths, dtype=jnp.int32)
    before = positions[:, None] >= doc_ends[None, :]
    doc_index = jnp.sum(before.astype(jnp.int32), axis=1, dtype=jnp.int32)
    doc_start = jnp.sum(jnp.where(before, lengths[None, :], 0), axis=1, dtype=jnp.int32)
    return (doc_index, positions - doc_start)


def rotate(vectors, offsets, factors):
    half_dim = vectors.shape[-1] // 2
    exponent = jnp.arange(half_dim, dtype=jnp.float32) * (2.0 / vectors.shape[-1])
    inverse = 1.0 / (factors * jnp.power(jnp.float32(THETA), exponent))
    angles = offsets.astype(jnp.float32)[:, None] * inverse[None, :]
    cosine = jnp.cos(angles)[:, None, :]
    sine_part = jnp.sin(angles)[:, None, :]
    first_half = vectors[..., :half_dim]
    second_half = vectors[..., half_dim:]
    return jnp.concatenate(
        [
            first_half * cosine - second_half * sine_part,
            second_half * cosine + first_half * sine_part,
        ],
        axis=-1,
    )


def source_table(owner_map):
    ctx_size = owner_map.shape[0]
    devices = jnp.arange(ctx_size, dtype=jnp.int32)
    matches = owner_map[None, :, :] == devices[:, None, None]
    return jnp.sum(jnp.where(matches, devices[None, :, None], 0), axis=1, dtype=jnp.int32)


def select(one_hot, payload):
    flattened = payload.reshape(one_hot.shape[1], -1)
    return jnp.dot(one_hot, flattened, preferred_element_type=jnp.float32).astype(jnp.bfloat16)


def attend_slots(q_slots, k_slots, v_slots, visible):
    slot_count, block_rows, kv_local, heads_here, head_dim = q_slots.shape
    span = k_slots.shape[1]
    score_scale = 1.0 / math.sqrt(head_dim)
    q_items = q_slots.transpose(0, 2, 3, 1, 4).reshape(
        slot_count * kv_local, heads_here * block_rows, head_dim
    )
    k_items = k_slots.transpose(0, 2, 1, 3).reshape(slot_count * kv_local, span, head_dim)
    v_items = v_slots.transpose(0, 2, 1, 3).reshape(slot_count * kv_local, span, head_dim)
    slot_of = jnp.arange(slot_count * kv_local, dtype=jnp.int32) // kv_local

    def attend_item(pieces):
        q_item, k_item, v_item, slot_number = pieces
        mask = lax.dynamic_index_in_dim(visible, slot_number, 0, keepdims=False)
        scores = (
            jnp.einsum("qd,kd->qk", q_item, k_item, preferred_element_type=jnp.float32)
            * score_scale
        )
        scores = scores.reshape(heads_here, block_rows, span)
        scores = jnp.where(mask[None], scores, -1e30)
        row_peak = jnp.max(scores, axis=2, keepdims=True)
        weights = jnp.exp(scores - row_peak)
        row_total = jnp.sum(weights, axis=2, keepdims=True)
        mixture = jnp.einsum(
            "hqk,kd->hqd", weights.astype(jnp.bfloat16), v_item, preferred_element_type=jnp.float32
        )
        return (mixture / row_total).astype(jnp.bfloat16)

    result = lax.map(attend_item, (q_items, k_items, v_items, slot_of))
    result = result.reshape(slot_count, kv_local, heads_here, block_rows, head_dim).transpose(
        0, 3, 1, 2, 4
    )
    return result.reshape(slot_count * block_rows, kv_local, heads_here, head_dim)


def local(queries, keys, values, rope_factors, doc_lengths, owner_map):
    ctx_size = lax.axis_size("ctx")
    ctx_index = lax.axis_index("ctx")
    row_count = queries.shape[0]
    per_dev = owner_map.shape[1]
    block_rows = row_count // per_dev
    tail_rows = row_count // 4
    span = tail_rows + block_rows
    head_dim = 2 * rope_factors.shape[0]
    kv_keys, kv_values = (
        lax.all_to_all(keys, "tp", split_axis=1, concat_axis=0, tiled=True),
        lax.all_to_all(values, "tp", split_axis=1, concat_axis=0, tiled=True),
    )
    kv_width = kv_keys.shape[1]
    kv_local = kv_width // head_dim
    q_local = queries.shape[1] // head_dim
    group_size = q_local // kv_local
    anchor = ctx_index * row_count + jnp.arange(row_count, dtype=jnp.int32)
    unused_docs, offs_anchor = doc_tables(doc_lengths, anchor)
    q_rot = rotate(
        queries.astype(jnp.float32).reshape(row_count, q_local, head_dim), offs_anchor, rope_factors
    ).astype(jnp.bfloat16)
    k_rot = rotate(
        kv_keys.astype(jnp.float32).reshape(row_count, kv_local, head_dim),
        offs_anchor,
        rope_factors,
    ).astype(jnp.bfloat16)
    k_rot = k_rot.reshape(row_count, kv_width)
    k_tail, v_tail = passed_along(
        (k_rot[row_count - tail_rows :], kv_values[row_count - tail_rows :]), "ctx", 1
    )
    k_ext = jnp.concatenate([k_tail, k_rot], axis=0)
    v_ext = jnp.concatenate([v_tail, kv_values], axis=0)
    k_windows = jnp.stack(
        [k_ext[slot * block_rows : slot * block_rows + span] for slot in range(per_dev)]
    )
    v_windows = jnp.stack(
        [v_ext[slot * block_rows : slot * block_rows + span] for slot in range(per_dev)]
    )
    devices = jnp.arange(ctx_size, dtype=jnp.int32)
    owner_row = lax.dynamic_index_in_dim(owner_map, ctx_index, 0, keepdims=False)
    send_pick = (owner_row[None, :] == devices[:, None]).astype(jnp.bfloat16)
    sources = source_table(owner_map)
    my_sources = lax.dynamic_index_in_dim(sources, ctx_index, 0, keepdims=False)
    take_slots = (my_sources[:, None] == devices[None, :]).astype(jnp.bfloat16)
    k_send = select(send_pick, k_windows).reshape(ctx_size, span, kv_width)
    v_send = select(send_pick, v_windows).reshape(ctx_size, span, kv_width)
    k_arrived, v_arrived = (
        lax.all_to_all(k_send, "ctx", split_axis=0, concat_axis=0, tiled=True),
        lax.all_to_all(v_send, "ctx", split_axis=0, concat_axis=0, tiled=True),
    )
    k_slots = select(take_slots, k_arrived).reshape(per_dev, span, kv_local, head_dim)
    v_slots = select(take_slots, v_arrived).reshape(per_dev, span, kv_local, head_dim)
    slot_start = my_sources * row_count + jnp.arange(per_dev, dtype=jnp.int32) * block_rows
    pos_q = slot_start[:, None] + jnp.arange(block_rows, dtype=jnp.int32)[None, :]
    pos_k = slot_start[:, None] - tail_rows + jnp.arange(span, dtype=jnp.int32)[None, :]
    doc_q, unused_q = doc_tables(doc_lengths, pos_q.reshape(-1))
    doc_k, unused_k = doc_tables(doc_lengths, pos_k.reshape(-1))
    doc_q = doc_q.reshape(per_dev, block_rows)
    doc_k = doc_k.reshape(per_dev, span)
    visible = (
        (doc_q[:, :, None] == doc_k[:, None, :])
        & (pos_k[:, None, :] <= pos_q[:, :, None])
        & (pos_k[:, None, :] >= 0)
    )
    q_send = select(send_pick, q_rot).reshape(ctx_size, block_rows, kv_local, group_size, head_dim)
    arrived = lax.all_to_all(q_send, "ctx", split_axis=0, concat_axis=0, tiled=True)
    heads_here = arrived.shape[3]
    q_slots = select(take_slots, arrived).reshape(
        per_dev, block_rows, kv_local, heads_here, head_dim
    )
    finished = attend_slots(q_slots, k_slots, v_slots, visible)
    return finished.reshape(row_count, q_local * head_dim)


def solution(mesh):
    in_specs = (P("ctx", "tp"), P(("ctx", "tp"), None), P(("ctx", "tp"), None), P(), P(), P())
    out_specs = P("ctx", "tp")
    return jax.shard_map(local, mesh=mesh, in_specs=in_specs, out_specs=out_specs, check_vma=False)
```

profile of v0, /device:TPU:0, one launch (start us, length us, event | category | flops | bytes accessed | tf_op | source)
XLA Modules:
  0.0 534.0 jit_solution(5519533580216134241)
XLA Ops:
  2.3 6.3 %all-to-all-start.1 = ((bf16[512,4,256]{2,0,1:T(8,128)(2,1)}), bf16[512,4,256]{2,0,1:T(8,128)(2,1)S(1)}, u32[]{:S(2)}, u32[]{:S(2)}) async-start(bf16[512,4,256]{2,0,1:T(8,128)(2,1)} %bitcast.135), calls=%async_computation.1 | async-start | bytes 2097152 | tf_op jit(solution)/shard_map/all_to_all | solution.py:100
  13.6 5.4 %multiply_cosine_fusion = (f32[2048,64]{1,0:T(8,128)S(1)}, f32[2048,64]{1,0:T(8,128)}) fusion(f32[64]{0:T(128)S(1)} %multiply_divide_fusion, f32[2048]{0:T(1024)S(1)} %subtract_convert_fusion.1), kind=kLoop, calls=%fused_computation.39 | loop fusion | flops 131072 | bytes 1057024 | tf_op jit(solution)/shard_map/cos | solution.py:30
  19.0 15.4 %all-to-all-done.1 = bf16[512,4,256]{2,0,1:T(8,128)(2,1)S(1)} async-done(((bf16[512,4,256]{2,0,1:T(8,128)(2,1)}), bf16[512,4,256]{2,0,1:T(8,128)(2,1)S(1)}, u32[]{:S(2)}, u32[]{:S(2)}) %all-to-all-start.1) | async-done | bytes 1048608 | tf_op jit(solution)/shard_map/all_to_all | solution.py:100
  34.3 4.2 all-to-all-start.3
  42.4 8.9 %multiply_subtract_fusion = (bf16[2048,2,64]{2,1,0:T(2,128)(2,1)S(1)}, bf16[2048,2,64]{2,1,0:T(2,128)(2,1)S(1)}) fusion(f32[2048,2,128]{2,1,0:T(2,128)S(1)} %reshape.327, f32[2048,64]{1,0:T(8,128)} %get-tuple-element.88, f32[2048,64]{1,0:T(8,128)S(1)} %get-tuple-element.87), kind=kLoop, calls=%fused_computation.36 | loop fusion | flops 2097152 | bytes 4194304 | tf_op jit(solution)/shard_map/sub | solution.py:36
  51.3 2.9 maximum_convert_fusion
  69.4 15.6 %stack.62 = bf16[8,196608]{1,0:T(8,128)(2,1)S(1)} concatenate(bf16[1,196608]{1,0:T(2,128)(2,1)} %bitcast.179, bf16[1,196608]{1,0:T(2,128)(2,1)} %bitcast.181, bf16[1,196608]{1,0:T(2,128)(2,1)} %stack.56, bf16[1,196608]{1,0:T(2,128)(2,1)} %stack.57, bf16[1,196608]{1,0:T(2,128)(2,1)} %stack.58, bf16[1,196608]{1,0:T(2,128)(2,1)} %stack.59, bf16[1,196608]{1,0:T(2,128)(2,1)} %stack.60, ...), dimensions={0} | concatenate | bytes 6291456 | tf_op jit(solution)/shard_map/stack | solution.py:123
  88.2 4.5 all-to-all-start.2
  93.8 3.6 collective-permute-start.1
  97.4 11.2 %convert_bitcast_fusion = f32[256,8,16,128]{3,1,2,0:T(8,128)} fusion(bf16[2048,2048]{1,0:T(8,128)(2,1)} %param.8), kind=kLoop, calls=%fused_computation.25 | loop fusion | flops 4194304 | bytes 25165824
  108.6 14.1 %copy.53 = f32[256,8,16,128]{3,2,1,0:T(8,128)} copy(f32[256,8,16,128]{3,1,2,0:T(8,128)} %convert_bitcast_fusion) | data formatting | bytes 33554432
  136.5 15.6 %stack.71 = bf16[8,196608]{1,0:T(8,128)(2,1)S(1)} concatenate(bf16[1,196608]{1,0:T(2,128)(2,1)} %bitcast.173, bf16[1,196608]{1,0:T(2,128)(2,1)} %bitcast.174, bf16[1,196608]{1,0:T(2,128)(2,1)} %bitcast.175, bf16[1,196608]{1,0:T(2,128)(2,1)} %bitcast.176, bf16[1,196608]{1,0:T(2,128)(2,1)} %bitcast.177, bf16[1,196608]{1,0:T(2,128)(2,1)} %bitcast.178, bf16[1,196608]{1,0:T(2,128)(2,1)} %bitcast.180, ...), dimensions={0} | concatenate | bytes 6291456 | tf_op jit(solution)/shard_map/stack | solution.py:126
  155.3 11.9 %all-to-all-start.4 = ((bf16[8,768,256]{2,1,0:T(8,128)(2,1)}), bf16[8,768,256]{2,1,0:T(8,128)(2,1)S(1)}, u32[]{:S(2)}, u32[]{:S(2)}) async-start(bf16[8,768,256]{2,1,0:T(8,128)(2,1)} %copy.48), calls=%async_computation.4 | async-start | bytes 6291456 | tf_op jit(solution)/shard_map/all_to_all | solution.py:139
  167.2 15.5 %subtract_convert_fusion = (bf16[2048,16,64]{2,1,0:T(8,128)(2,1)S(1)}, bf16[2048,16,64]{2,1,0:T(8,128)(2,1)S(1)}) fusion(f32[2048,16,128]{2,1,0:T(8,128)} %bitcast.157, f32[2048,64]{1,0:T(8,128)} %get-tuple-element.88, f32[2048,64]{1,0:T(8,128)} %copy-done), kind=kLoop, calls=%fused_computation.27 | loop fusion | flops 16777216 | bytes 26214400 | tf_op jit(solution)/shard_map/convert.3
  182.8 6.1 %pad_maximum_fusion = bf16[2048,16,128]{2,1,0:T(8,128)(2,1)} fusion(bf16[2048,16,64]{2,1,0:T(8,128)(2,1)S(1)} %get-tuple-element.66, bf16[2048,16,64]{2,1,0:T(8,128)(2,1)S(1)} %get-tuple-element.65), kind=kLoop, calls=%fused_computation.30 | loop fusion | flops 16777216 | bytes 16777216 | tf_op jit(solution)/shard_map/concatenate | solution.py:34
  188.9 10.1 %convert_element_type.69 = bf16[8,524288]{1,0:T(8,128)(2,1)} reshape(bf16[2048,16,128]{2,1,0:T(8,128)(2,1)} %pad_maximum_fusion) | data formatting | bytes 16777216 | tf_op jit(solution)/shard_map/convert_element_type | solution.py:111
  199.0 9.1 %convolution_convert_fusion.1 = bf16[8,524288]{1,0:T(8,128)(2,1)} fusion(bf16[8,524288]{1,0:T(8,128)(2,1)} %convert_element_type.69, s32[8]{0:T(128)S(1)} %dynamic-slice_bitcast_fusion.1), kind=kOutput, calls=%fused_computation.20 | convolution fusion | flops 71303232 | bytes 16777248 | tf_op jit(solution)/shard_map/dot_general | solution.py:52
  208.1 7.7 %copy.40 = bf16[8,256,2,8,128]{4,3,2,1,0:T(8,128)(2,1)} copy(bf16[8,256,2,8,128]{4,0,3,2,1:T(8,128)(2,1)} %bitcast.159) | data formatting | bytes 16777216 | tf_op jit(solution)/shard_map/reshape | solution.py:155
  215.8 4.9 all-to-all-start
  221.2 3.6 and_and_fusion
  224.8 3.7 copy.59
  229.5 2.5 copy.44
  234.8 2.5 copy.49
  237.3 77.6 %all-to-all-done = bf16[8,256,2,8,128]{4,3,2,1,0:T(8,128)(2,1)} async-done(((bf16[8,256,2,8,128]{4,3,2,1,0:T(8,128)(2,1)}), bf16[8,256,2,8,128]{4,3,2,1,0:T(8,128)(2,1)}, u32[]{:S(2)}, u32[]{:S(2)}) %all-to-all-start) | async-done | bytes 8388640 | tf_op jit(solution)/shard_map/all_to_all | solution.py:156
  314.8 11.8 %convolution_convert_fusion = bf16[8,524288]{1,0:T(8,128)(2,1)} fusion(bf16[1,8,4096,128]{3,2,1,0:T(8,128)(2,1)} %bitcast.41, s32[8]{0:T(128)S(1)} %get-tuple-element.60), kind=kOutput, calls=%fused_computation.19 | convolution fusion | flops 71303232 | bytes 16777248 | tf_op jit(solution)/shard_map/dot_general | solution.py:52
  326.6 12.0 %copy.41 = bf16[8,2,8,256,128]{4,3,2,1,0:T(8,128)(2,1)} copy(bf16[8,2,8,256,128]{4,0,2,1,3:T(8,128)(2,1)} %bitcast.160) | data formatting | bytes 16777216 | tf_op jit(solution)/shard_map/transpose | solution.py:59
  338.6 169.9 %while.10 = (s32[]{:T(128)}, bf16[16,8,256,128]{3,2,1,0:T(8,128)(2,1)}, s32[16]{0:T(128)S(1)}, pred[8,256,768]{2,1,0:T(8,128)(4,1)}, bf16[16,2048,128]{2,1,0:T(8...) while((s32[]{:T(128)}, ...), condition=%wide.region_8.9_spmd, body=%wide.region_5.8_spmd.sunk | while | flops 818409472 | bytes 21153944 | solution.py:83
  341.7 2.4 fusion.39
  346.5 2.7 fusion.41
  352.4 2.4 fusion.39
  354.8 2.3 fusion.40
  357.1 2.7 fusion.41
  363.0 2.4 fusion.39
  365.4 2.3 fusion.40
  367.7 2.7 fusion.41
  373.6 2.4 fusion.39
  378.3 2.7 fusion.41
  384.2 2.4 fusion.39
  388.9 2.7 fusion.41
  394.8 2.4 fusion.39
  397.2 2.3 fusion.40
  399.5 2.7 fusion.41
  405.4 2.4 fusion.39
  410.1 2.7 fusion.41
  416.0 2.4 fusion.39
  420.7 2.7 fusion.41
  426.6 2.4 fusion.39
  431.3 2.7 fusion.41
  437.2 2.4 fusion.39
  441.9 2.7 fusion.41
  447.8 2.4 fusion.39
  452.5 2.7 fusion.41
  458.4 2.4 fusion.39
  463.1 2.7 fusion.41
  469.0 2.4 fusion.39
  473.7 2.7 fusion.41
  479.6 2.4 fusion.39
  484.3 2.7 fusion.41
  490.2 2.4 fusion.39
  494.9 2.7 fusion.41
  500.8 2.4 fusion.39
  505.5 2.7 fusion.41
  508.5 12.0 %copy.77 = bf16[8,2,8,256,128]{4,2,1,3,0:T(8,128)(2,1)} copy(bf16[8,2,8,256,128]{4,3,2,1,0:T(8,128)(2,1)} %bitcast.172) | data formatting | bytes 16777216 | tf_op jit(solution)/shard_map/reshape | solution.py:84
  520.5 13.3 %reshape_reshape.3 = bf16[2048,2048]{1,0:T(8,128)(2,1)} reshape(bf16[8,256,2,8,128]{4,3,2,1,0:T(8,128)(2,1)} %bitcast.161) | data formatting | bytes 16777216 | tf_op jit(solution)/shard_map/reshape;reshape | solution.py:162
  (131 shorter events, 106.0 us)
Async XLA Ops:
  0.0 13.4 %copy-start.1 = (s32[64]{0:T(128)S(1)}, s32[64]{0:T(128)}, u32[]{:S(2)}) copy-start(s32[64]{0:T(128)} %param.12) | copy-start | bytes 772
  0.0 13.6 %copy-start.2 = (f32[64]{0:T(128)S(1)}, f32[64]{0:T(128)}, u32[]{:S(2)}) copy-start(f32[64]{0:T(128)} %param.11) | copy-start | bytes 772
  2.3 32.0 %all-to-all-start.1 = ((bf16[512,4,256]{2,0,1:T(8,128)(2,1)}), bf16[512,4,256]{2,0,1:T(8,128)(2,1)S(1)}, u32[]{:S(2)}, u32[]{:S(2)}) async-start(bf16[512,4,256]{2,0,1:T(8,128)(2,1)} %bitcast.135), calls=%async_computation.1 | async-start | bytes 2097152 | tf_op jit(solution)/shard_map/all_to_all | solution.py:100
  19.0 32.3 %copy-start = (f32[2048,64]{1,0:T(8,128)}, f32[2048,64]{1,0:T(8,128)S(1)}, u32[]{:S(2)}) copy-start(f32[2048,64]{1,0:T(8,128)S(1)} %get-tuple-element.87) | copy-start | bytes 1572868
  34.3 53.9 %all-to-all-start.3 = ((bf16[512,4,256]{0,2,1:T(8,128)(2,1)}), bf16[512,4,256]{0,2,1:T(8,128)(2,1)}, u32[]{:S(2)}, u32[]{:S(2)}) async-start(bf16[512,4,256]{0,2,1:T(8,128)(2,1)} %bitcast.21), calls=%async_computation.3 | async-start | bytes 2097152 | tf_op jit(solution)/shard_map/all_to_all | solution.py:101
  55.1 10.1 %collective-permute-start = (bf16[512,256]{1,0:T(8,128)(2,1)}, bf16[512,256]{1,0:T(8,128)(2,1)}, u32[]{:S(2)}, u32[]{:S(2)}) collective-permute-start(bf16[512,256]{1,0:T(8,128)(2,1)} %bitcast.136), channel_id=1, source_target_pairs={{0,4},{4,8},{8,12},{12,16},{16,20},{20,24},{24,28},{1,5},{5,9},{9,... | collective-permute-start | bytes 786440 | tf_op jit(solution)/shard_map/ppermute | solution.py:14
  88.2 67.1 %all-to-all-start.2 = ((bf16[8,768,256]{2,1,0:T(8,128)(2,1)}), bf16[8,768,256]{2,1,0:T(8,128)(2,1)}, u32[]{:S(2)}, u32[]{:S(2)}) async-start(bf16[8,768,256]{2,1,0:T(8,128)(2,1)} %copy.43), calls=%async_computation.2 | async-start | bytes 6291456 | tf_op jit(solution)/shard_map/all_to_all | solution.py:138
  93.8 30.4 %collective-permute-start.1 = (bf16[512,256]{1,0:T(8,128)(2,1)S(1)}, bf16[512,256]{1,0:T(8,128)(2,1)S(1)}, u32[]{:S(2)}, u32[]{:S(2)}) collective-permute-start(bf16[512,256]{1,0:T(8,128)(2,1)S(1)} %bitcast.186), channel_id=1, source_target_pairs={{0,4},{4,8},{8,12},{12,16},{16,20},{20,24},{24,28},{1,5},{5,9},{9,... | collective-permute-start | bytes 786440 | tf_op jit(solution)/shard_map/ppermute | solution.py:14
  155.3 60.5 %all-to-all-start.4 = ((bf16[8,768,256]{2,1,0:T(8,128)(2,1)}), bf16[8,768,256]{2,1,0:T(8,128)(2,1)S(1)}, u32[]{:S(2)}, u32[]{:S(2)}) async-start(bf16[8,768,256]{2,1,0:T(8,128)(2,1)} %copy.48), calls=%async_computation.4 | async-start | bytes 6291456 | tf_op jit(solution)/shard_map/all_to_all | solution.py:139
  215.8 99.0 %all-to-all-start = ((bf16[8,256,2,8,128]{4,3,2,1,0:T(8,128)(2,1)}), bf16[8,256,2,8,128]{4,3,2,1,0:T(8,128)(2,1)}, u32[]{:S(2)}, u32[]{:S(2)}) async-start(bf16[8,256,2,8,128]{4,3,2,1,0:T(8,128)(2,1)} %copy.40), calls=%async_computation | async-start | bytes 16777216 | tf_op jit(solution)/shard_map/all_to_all | solution.py:156
where the time goes:
time: 545 us; the launch traced here: 534 us
  local copies, waits for them, and re-layouts  175 us (32%)
  matrix products  107 us (20%)
  other arithmetic  94.1 us (17%)
  waiting for transfers between devices  93 us (17%)
  starting transfers between devices  37.6 us (7%)
  loops' own time  26.8 us (5%)
    all_to_all x1, waiting for transfers between devices, local(): lax.all_to_all(q_send, 'ctx', split_axis=0, concat_axis=0, tiled=True)  77.6 us
    dot_general x16, matrix products, attend_item(): jnp.einsum('hqk,kd->hqd', weights.astype(jnp.bfloat16), v_item, preferred...  43.4 us
    dot_general x16, matrix products, attend_item(): jnp.einsum('qd,kd->qk', q_item, k_item, preferred_element_type=jnp.float32)  38.6 us
    unnamed x24, local copies, waits for them, and re-layouts  38.5 us
    reduce_sum x16, other arithmetic, attend_item(): row_total = jnp.sum(weights, axis=2, keepdims=True)  37.1 us
    another operation x1, loops' own time, attend_slots(): result = lax.map(attend_item, (q_items, k_items, v_items, slot_of))  26.8 us
    dot_general x6, matrix products, select(): jnp.dot(one_hot, flattened, preferred_element_type=jnp.float32)  24.9 us
    another operation x7, local copies, waits for them, and re-layouts, local(): jnp.stack([k_ext[slot * block_rows:slot * block_rows + span] for slot in...  21.8 us
  transfers between devices with their start and end apart: 7, of which 2 were waited for; matrix products, arithmetic and copies ran while one was open for 34% of the time, Pallas kernels for 0%

commit v1 on v0

v1 whole, which is shorter than its diff:
```python
import functools
import math

import jax
import jax.numpy as jnp
from jax import lax
from jax.experimental import pallas as pl
from jax.experimental.pallas import tpu as pltpu
from jax.sharding import PartitionSpec as P

THETA = 500000.0
BLOCK = 256
LANES = 128
MESH = pl.DeviceIdType.MESH


def flip(index, by, count):
    out, bit = 0, 1
    while bit < count:
        out = out + ((index // bit + by // bit) % 2) * bit
        bit *= 2
    return out


def turn(x, cosine, sine):
    return x * cosine + pltpu.roll(x, LANES // 2, 1) * sine


def fused_kernel(
    n, tp, kv_local, group, halo,
    lengths_ref, pick_ref, inv_ref, q_hbm, k_ref, v_hbm,
    land,
    qbuf, krot, kwins, vwins, cos_ref, sin_ref, start_ref, bias_ref, outbuf,
    kv_send, kv_recv, halo_send, halo_recv, out_send, out_recv, q_sem,
):
    c = lax.axis_index("ctx")
    t = lax.axis_index("tp")
    blocks = qbuf.shape[0]
    shard = k_ref.shape[0]
    rows = blocks * BLOCK
    span = halo + 1
    docs = lengths_ref.shape[0]
    after = (c + 1) % n

    barrier = pltpu.get_barrier_semaphore()
    for j in range(1, tp):
        pl.semaphore_signal(barrier, inc=1, device_id={"tp": (t + j) % tp}, device_id_type=MESH)
    for j in range(1, n):
        pl.semaphore_signal(barrier, inc=1, device_id={"ctx": (c + j) % n}, device_id_type=MESH)
    q_copy = pltpu.make_async_copy(q_hbm, qbuf, q_sem)
    q_copy.start()
    pl.semaphore_wait(barrier, tp + n - 2)

    def kv_copy(kind, g, j):
        peer = (t + j) % tp
        head = peer * kv_local + g
        if kind == 0:
            src, dst = krot.at[head], kwins[g]
        else:
            column = pl.multiple_of(head * LANES, LANES)
            src, dst = v_hbm.at[:, :, pl.ds(column, LANES)], vwins[g]
        dst = dst.at[pl.ds(halo + t * shard, shard)]
        if j == 0:
            return pltpu.make_async_copy(src, dst, kv_recv.at[kind, g, 0])
        return pltpu.make_async_remote_copy(
            src_ref=src, dst_ref=dst, send_sem=kv_send.at[kind, g, j],
            recv_sem=kv_recv.at[kind, g, j], device_id={"tp": peer}, device_id_type=MESH,
        )

    def halo_copy(kind, g):
        win = (kwins, vwins)[kind][g]
        return pltpu.make_async_remote_copy(
            src_ref=win.at[pl.ds(blocks, halo)], dst_ref=win.at[pl.ds(0, halo)],
            send_sem=halo_send.at[kind, g], recv_sem=halo_recv.at[kind, g],
            device_id={"ctx": after}, device_id_type=MESH,
        )

    def send_kv(kind, g):
        for j in range(tp):
            kv_copy(kind, g, j).start()

    def pass_halo(g):
        for kind in (1, 0):
            kv_copy(kind, g, 0).wait()
            for j in range(1, tp):
                kv_copy(kind, g, j).wait_recv()
        for kind in (1, 0):
            halo_copy(kind, g).start()

    send_kv(1, 0)

    lane = lax.broadcasted_iota(jnp.int32, (BLOCK, LANES), 1)
    line = lax.broadcasted_iota(jnp.int32, (BLOCK, LANES), 0)

    def tables(i, carry):
        b = (t * shard + i) % blocks
        at = c * rows + b * BLOCK + line

        def one(d, state):
            end, start = state
            end = end + lengths_ref[d]
            return end, jnp.where(at >= end, end, start)

        end, start = lax.fori_loop(0, docs, one, (jnp.int32(0), jnp.zeros_like(at)))
        angle = (at - start).astype(jnp.float32) * inv_ref[...]
        sine = jnp.sin(angle)
        cos_ref[b] = jnp.cos(angle)
        sin_ref[b] = jnp.where(lane < LANES // 2, -sine, sine)
        start_ref[b] = start - c * rows
        return carry

    lax.fori_loop(0, shard, tables, 0)

    def turn_keys(i, carry):
        b = t * shard + i
        for head in range(tp * kv_local):
            x = k_ref[i, :, head * LANES:(head + 1) * LANES].astype(jnp.float32)
            krot[head, i] = turn(x, cos_ref[b], sin_ref[b]).astype(jnp.bfloat16)
        return carry

    lax.fori_loop(0, shard, turn_keys, 0)
    send_kv(0, 0)
    for g in range(1, kv_local):
        send_kv(1, g)
        send_kv(0, g)
    lax.fori_loop(shard, blocks, tables, 0)

    q_copy.wait()
    step_rows = BLOCK // 4

    def turn_queries(i, carry):
        b = i // 4
        part = pl.ds(pl.multiple_of((i % 4) * step_rows, step_rows), step_rows)
        cosine, sine = cos_ref[b, part, :], sin_ref[b, part, :]
        for head in range(kv_local * group):
            cols = slice(head * LANES, (head + 1) * LANES)
            x = qbuf[b, part, cols].astype(jnp.float32)
            qbuf[b, part, cols] = turn(x, cosine, sine).astype(jnp.bfloat16)
        return carry

    lax.fori_loop(0, blocks * 4, turn_queries, 0)

    factor = math.log2(math.e) / math.sqrt(LANES)
    pairs = n // 2 - 1

    def out_copy(g, s):
        if isinstance(s, int) and s == 0:
            return pltpu.make_async_copy(outbuf.at[g, 0], land.at[g, 0], out_recv.at[g, 0])
        return pltpu.make_async_remote_copy(
            src_ref=outbuf.at[g, s], dst_ref=land.at[g, s], send_sem=out_send.at[g, s],
            recv_sem=out_recv.at[g, s], device_id={"ctx": flip(c, s, n)}, device_id_type=MESH,
        )

    pass_halo(0)
    for g in range(kv_local):
        for kind in (1, 0):
            halo_copy(kind, g).wait_recv()

        def step(i, carry, g=g):
            far = 2 * (i % pairs + 1) + i // pairs
            s = jnp.where(i < 2 * pairs, far, n - 1 - i)
            r = pick_ref[s]
            start = start_ref[r]
            own = r * BLOCK + line
            for tile in range(span * BLOCK // LANES):
                at = (r - halo) * BLOCK + tile * LANES + lane
                seen = (at >= start) & (at <= own)
                bias_ref[:, tile * LANES:(tile + 1) * LANES] = jnp.where(seen, 0.0, -1e30)
            k_win = kwins[g][pl.ds(r, span)].reshape(span * BLOCK, LANES)
            v_win = vwins[g][pl.ds(r, span)].reshape(span * BLOCK, LANES)
            for h in range(group):
                q = qbuf[r, :, (g * group + h) * LANES:(g * group + h + 1) * LANES]
                scores = lax.dot_general(
                    q, k_win, (((1,), (1,)), ((), ())), preferred_element_type=jnp.float32
                ) + bias_ref[...]
                peak = jnp.max(scores, axis=1, keepdims=True)
                weight = jnp.exp2((scores - peak) * factor)
                total = jnp.sum(weight, axis=1, keepdims=True)
                mixed = jnp.dot(
                    weight.astype(jnp.bfloat16), v_win, preferred_element_type=jnp.float32
                )
                outbuf[g, s, :, h * LANES:(h + 1) * LANES] = (mixed * (1.0 / total)).astype(
                    jnp.bfloat16
                )

            @pl.when(i < n - 1)
            def _():
                out_copy(g, s).start()

            if g + 1 < kv_local:
                @pl.when(i == n // 2)
                def _():
                    pass_halo(g + 1)

            return carry

        lax.fori_loop(0, n, step, 0)
        out_copy(g, 0).start()

    for g in range(kv_local):
        for kind in (1, 0):
            for j in range(1, tp):
                kv_copy(kind, g, j).wait_send()
            halo_copy(kind, g).wait_send()
        out_copy(g, 0).wait()

        def finish(s, carry, g=g):
            out_copy(g, s).wait()
            return carry

        lax.fori_loop(1, n, finish, 0)


def place_kernel(where_ref, land_ref, out_ref):
    out_ref[...] = land_ref[0, 0]


def local(n, tp, queries, keys, values, rope_factors, doc_lengths, owner_map):
    c = lax.axis_index("ctx")
    rows, q_width = queries.shape
    blocks = owner_map.shape[1]
    head_dim = 2 * rope_factors.shape[0]
    kv_heads = keys.shape[1] // head_dim
    kv_local = kv_heads // tp
    group = q_width // head_dim // kv_local
    shard = keys.shape[0] // BLOCK
    halo = rows // 4 // BLOCK
    width = group * head_dim

    exponent = jnp.arange(head_dim // 2, dtype=jnp.float32) * (2.0 / head_dim)
    inverse = 1.0 / (rope_factors * jnp.power(jnp.float32(THETA), exponent))
    inverse = jnp.concatenate([inverse, inverse])[None, :]
    steps = jnp.arange(n, dtype=jnp.int32)
    partner = c ^ steps
    mine = lax.dynamic_index_in_dim(owner_map, c, 0, keepdims=False)
    slots = jnp.arange(blocks, dtype=jnp.int32)
    pick = jnp.sum(jnp.where(mine[None, :] == partner[:, None], slots[None, :], 0), axis=1)
    source = jnp.sum(jnp.where(owner_map == c, steps[:, None], 0), axis=0)
    where = c ^ source

    vmem = pl.BlockSpec(memory_space=pltpu.VMEM)
    smem = pl.BlockSpec(memory_space=pltpu.SMEM)
    anywhere = pl.BlockSpec(memory_space=pl.ANY)
    window = pltpu.VMEM((halo + blocks, BLOCK, LANES), jnp.bfloat16)
    table = pltpu.VMEM((blocks, BLOCK, LANES), jnp.float32)
    dma = pltpu.SemaphoreType.DMA
    landed = pl.pallas_call(
        functools.partial(fused_kernel, n, tp, kv_local, group, halo),
        out_shape=jax.ShapeDtypeStruct((kv_local, n, BLOCK, width), jnp.bfloat16),
        in_specs=[smem, smem, vmem, anywhere, vmem, anywhere],
        out_specs=anywhere,
        scratch_shapes=[
            pltpu.VMEM((blocks, BLOCK, q_width), jnp.bfloat16),
            pltpu.VMEM((kv_heads, shard, BLOCK, LANES), jnp.bfloat16),
            [window] * kv_local,
            [window] * kv_local,
            table,
            table,
            pltpu.VMEM((blocks, BLOCK, LANES), jnp.int32),
            pltpu.VMEM((BLOCK, (halo + 1) * BLOCK), jnp.float32),
            pltpu.VMEM((kv_local, n, BLOCK, width), jnp.bfloat16),
            dma((2, kv_local, tp)),
            dma((2, kv_local, tp)),
            dma((2, kv_local)),
            dma((2, kv_local)),
            dma((kv_local, n)),
            dma((kv_local, n)),
            dma,
        ],
        compiler_params=pltpu.CompilerParams(
            collective_id=0, has_side_effects=True, vmem_limit_bytes=52 * 2**20
        ),
        name="attend_and_send",
    )(
        doc_lengths,
        pick.astype(jnp.int32),
        inverse,
        queries.reshape(blocks, BLOCK, q_width),
        keys.reshape(shard, BLOCK, kv_heads * head_dim),
        values.reshape(shard, BLOCK, kv_heads * head_dim),
    )
    return pl.pallas_call(
        place_kernel,
        grid_spec=pltpu.PrefetchScalarGridSpec(
            num_scalar_prefetch=1,
            grid=(blocks, kv_local),
            in_specs=[
                pl.BlockSpec((1, 1, BLOCK, width), lambda b, g, where: (g, where[b], 0, 0))
            ],
            out_specs=pl.BlockSpec((BLOCK, width), lambda b, g, where: (b, g)),
        ),
        out_shape=jax.ShapeDtypeStruct((rows, q_width), jnp.bfloat16),
        name="place_blocks",
    )(where.astype(jnp.int32), landed)


def solution(mesh):
    n, tp = mesh.shape["ctx"], mesh.shape["tp"]
    in_specs = (P("ctx", "tp"), P(("ctx", "tp"), None), P(("ctx", "tp"), None), P(), P(), P())
    return jax.shard_map(
        functools.partial(local, n, tp),
        mesh=mesh, in_specs=in_specs, out_specs=P("ctx", "tp"), check_vma=False,
    )
```

time: 545 us -> 161 us (0.30)
  the two profiles are of different devices: /device:TPU:0 before, /device:TPU:9 now
where the time goes in v1:
time: 161 us
  Pallas kernels  156 us (97%)
  local copies, waits for them, and re-layouts  2.57 us (2%)
  other arithmetic  2.13 us (1%)
    pallas_call x1, Pallas kernels, local(): pl.pallas_call(functools.partial(fused_kernel, n, tp, kv_local, group, ha...  143 us
    pallas_call x1, Pallas kernels, local(): pl.pallas_call(place_kernel, grid_spec=pltpu.PrefetchScalarGridSpec(num_s...  12.6 us

profile of v1, /device:TPU:9, one launch (start us, length us, event | category | flops | bytes accessed | tf_op | source)
XLA Modules:
  0.0 160.6 jit_solution(16290046213640704360)
XLA Ops:
  0.0 0.7 dynamic-slice_bitcast_fusion
  0.7 0.7 multiply_divide_fusion
  1.4 0.1 maximum_bitcast_fusion.inv_ref
  1.4 0.7 select_reduce_fusion.1
  2.2 0.5 iota_xor_fusion
  2.6 0.2 select_reduce_fusion.pick_ref
  2.8 0.0 copy-start
  2.8 1.2 copy-done
  4.0 0.0 copy-start.1
  4.0 0.7 copy-done.1
  4.7 143.4 %attend_and_send.1.land_ref = bf16[2,8,256,1024]{3,2,1,0:T(8,128)(2,1)} custom-call(s32[64]{0:T(128)S(1)} %copy-done.1, s32[8]{0:T(128)S(1)} %select_reduce_fusion.pick_ref, f32[1,128]{1,0:T(1,128)S(1)} %maximum_bitcast_fusion.inv_ref, bf16[8,256,2048]{2,1,0:T(8,128)(2,1)} %bitcast.8, bf16[2,256,1024]{2,1,0:T(8,128)(2,1)S(1)} %bitcast.7, ...), custom_call_target="tpu_custom_call" | custom-call | tf_op jit(solution)/shard_map/attend_and_send/pallas_call | solution.py:247
  148.1 12.6 %place_blocks.1 = bf16[2048,2048]{1,0:T(8,128)(2,1)} custom-call(s32[8]{0:T(128)} %get-tuple-element.6.where_ref, bf16[2,8,256,1024]{3,2,1,0:T(8,128)(2,1)} %attend_and_send.1.land_ref), custom_call_target="tpu_custom_call" | custom-call | tf_op jit(solution)/shard_map/place_blocks/pallas_call | solution.py:282
Async XLA Ops:
  2.8 1.2 copy-start
  4.0 0.7 copy-start.1
